TPU v7x, 32 devices: a whole 2x2x4 slice. The times are simulated.
32 devices in a mesh: req: 8 (over y, x, core), cache: 4 (over z).
Axes of the slice: x: 2, y: 2, z: 4, core: 2. Of those that a mesh axis runs over, the one named last changes fastest.
Arguments:
- cand_x: bfloat16 [8192, 1024], P(('req', 'cache')), may hold values from -6 to 6
- cand_req: int32 [8192, 1], P(('req', 'cache')), may hold values from 0 to 31; in each aligned block of 256 rows (0 to 255, 256 to 511, ...) at most 16 rows name the same one
- hist_len: int32 [32], P(('req', 'cache')), may hold values from 1 to 2048, 32768 in all
- block_place: int32 [32, 128], P(('req', 'cache')), may hold values from 0 to 127, each once within a row
- kv_store: bfloat16 [32, 32, 4, 16, 2048], P(('req', 'cache')), may hold values from -6 to 6
- store_bucket: int32 [32, 32, 4, 16], P(('req', 'cache')), may hold values from 1 to 127
- w_proj: bfloat16 [1024, 2048], replicated, may hold values from -0.1875 to 0.1875
- w_out: bfloat16 [1024, 1024], replicated, may hold values from -0.1875 to 0.1875
- time_bias: float32 [8, 128], replicated, may hold values from -4 to 4
Outputs:
- scored: bfloat16 [8192, 1024], P(('req', 'cache'))
Inputs may be any that keep to these rules, and one draw needn't show every extreme that they name: `cand_req`: among the 256 candidate rows of one device at most 16 belong to one request, and some request of some device has exactly 16. `hist_len`: the lengths sum to 32768. `block_place`: each row is a permutation of 0 to 127.
All inputs are finite; a program needn't handle non-finite values. No bound on the sum of `hist_len` on one device may be relied on, other than what follows from the above.
Results may differ from a plain program's by a relative error of at most 0.0055.
Values may be sent and summed in bfloat16 or wider, within the bound.
A program may use at most 128 MiB of HBM per device.

v0:
```python
import math

import jax
import jax.numpy as jnp
from jax import lax
from jax.sharding import PartitionSpec as P


def layer_norm(values):
    average = jnp.mean(values, axis=-1, keepdims=True)
    centred = values - average
    spread = jnp.mean(centred * centred, axis=-1, keepdims=True)
    return centred * lax.rsqrt(spread + 1e-05)


def prepare(inputs, w_proj):
    normed = layer_norm(inputs.astype(jnp.float32)).astype(jnp.bfloat16)
    return jax.nn.silu(jnp.dot(normed, w_proj, preferred_element_type=jnp.float32)).astype(
        jnp.bfloat16
    )


def send_back(update):
    return lax.all_to_all(update, ("req", "cache"), split_axis=0, concat_axis=0, tiled=True)


def shards(
    cand_x, cand_req, hist_len, block_place, kv_store, store_bucket, w_proj, w_out, time_bias
):
    devices = lax.axis_size(("req", "cache"))
    row_count = cand_x.shape[0]
    features = cand_x.shape[1]
    head_count = time_bias.shape[0]
    head_dim = features // head_count
    bucket_count = time_bias.shape[1]
    per_owner = kv_store.shape[2]
    block_ev = kv_store.shape[3]
    capacity = max(2, 2 * row_count // devices)
    arrived, arrived_bucket = (
        lax.all_to_all(kv_store, ("req", "cache"), split_axis=1, concat_axis=0, tiled=True),
        lax.all_to_all(store_bucket, ("req", "cache"), split_axis=1, concat_axis=0, tiled=True),
    )
    event_count = devices * per_owner * block_ev
    events = arrived.reshape(event_count, 2 * features)
    buckets = arrived_bucket.reshape(event_count)
    places = block_place[0]
    block_count = places.shape[0]
    block_ids = jnp.arange(block_count, dtype=jnp.int32)
    match = (places[:, None] == block_ids[None, :]).astype(jnp.int32)
    block_of_place = jnp.sum(match * block_ids[:, None], axis=0)
    position = (
        block_of_place[:, None] * block_ev + jnp.arange(block_ev, dtype=jnp.int32)[None, :]
    ).reshape(event_count)
    live = (position < hist_len[0]).astype(jnp.float32)
    bucket_table = (buckets[None, :] == jnp.arange(bucket_count, dtype=jnp.int32)[:, None]).astype(
        jnp.float32
    )
    bias = jnp.dot(time_bias, bucket_table, precision=lax.Precision.HIGHEST)
    score_scale = 1.0 / math.sqrt(head_dim)
    target = cand_req[:, 0]
    onehot = (target[:, None] == jnp.arange(devices, dtype=jnp.int32)[None, :]).astype(jnp.int32)
    earlier = jnp.cumsum(onehot, axis=0) - onehot
    slot_rank = jnp.sum(earlier * onehot, axis=1)
    flat_slot = target * capacity + slot_rank
    empty = jnp.zeros((devices * capacity, cand_x.shape[1]), cand_x.dtype)
    received = lax.all_to_all(
        empty.at[flat_slot].set(cand_x).reshape(devices, capacity, cand_x.shape[1]),
        ("req", "cache"),
        split_axis=0,
        concat_axis=0,
        tiled=True,
    )
    senders = received.shape[0]
    item_count = received.shape[1]
    flat_rows = received.reshape(senders * item_count, features)
    projected = prepare(flat_rows, w_proj)
    slot_count = projected.shape[0]
    gate_u = projected[:, :features]
    query = projected[:, features:]

    def one_head(head_index):
        start = head_index * head_dim
        query_head = lax.dynamic_slice_in_dim(query, start, head_dim, 1)
        key_head = lax.dynamic_slice_in_dim(events, start, head_dim, 1)
        value_head = lax.dynamic_slice_in_dim(events, features + start, head_dim, 1)
        bias_head = lax.dynamic_slice_in_dim(bias, head_index, 1, 0)
        scores = lax.dot_general(
            query_head, key_head, (((1,), (1,)), ((), ())), preferred_element_type=jnp.float32
        )
        weight = (jax.nn.silu(scores * score_scale + bias_head) * live[None, :]).astype(
            jnp.bfloat16
        )
        return jnp.dot(weight, value_head, preferred_element_type=jnp.float32)

    per_head = lax.map(one_head, jnp.arange(head_count, dtype=jnp.int32))
    attended = jnp.transpose(per_head, (1, 0, 2)).reshape(slot_count, features)
    hidden = (layer_norm(attended) * gate_u.astype(jnp.float32)).astype(jnp.bfloat16)
    update = (
        jnp.dot(hidden, w_out, preferred_element_type=jnp.float32)
        .astype(jnp.bfloat16)
        .reshape(senders, item_count, features)
    )
    returned = send_back(update)
    update = returned.reshape(devices * capacity, features)[flat_slot]
    return (cand_x.astype(jnp.float32) + update.astype(jnp.float32)).astype(jnp.bfloat16)


def solution(mesh):
    placed = (
        P(("req", "cache"), None),
        P(("req", "cache"), None),
        P(("req", "cache")),
        P(("req", "cache"), None),
        P(("req", "cache"), None, None, None, None),
        P(("req", "cache"), None, None, None),
        P(),
        P(),
        P(),
    )
    return jax.shard_map(
        shards, mesh=mesh, in_specs=placed, out_specs=P(("req", "cache"), None), check_vma=False
    )
```

profile of v0, /device:TPU:9, one launch (start us, length us, event | category | flops | bytes accessed | tf_op | source)
XLA Modules:
  0.0 334.0 jit_solution(4855702224858234160)
XLA Ops:
  0.0 1.6 copy.20
  1.6 6.4 %all-to-all-start.2 = ((s32[1,32,4,16]{3,2,0,1:T(4,128)}), s32[1,32,4,16]{3,2,0,1:T(4,128)S(1)}, u32[]{:S(2)}, u32[]{:S(2)}) async-start(s32[1,32,4,16]{3,2,0,1:T(4,128)} %copy.20), calls=%async_computation.2 | async-start | bytes 131072 | tf_op jit(solution)/shard_map/all_to_all | solution.py:41
  10.9 3.2 scatter_custom_fusion
  14.1 30.5 %all_to_all.28 = bf16[32,16,1024]{2,1,0:T(8,128)(2,1)S(1)} all-to-all(bf16[32,16,1024]{2,1,0:T(8,128)(2,1)} %bitcast.77), channel_id=1, replica_groups=mesh['req'=8,'cache'=4] {'req','cache'}, dimensions={0} | all-to-all | bytes 2097152 | tf_op jit(solution)/shard_map/all_to_all | solution.py:66
  44.7 4.9 %all-to-all-start.1 = ((bf16[1,32,4,16,2048]{4,3,2,0,1:T(8,128)(2,1)}), bf16[1,32,4,16,2048]{4,3,2,0,1:T(8,128)(2,1)}, u32[]{:S(2)}, u32[]{:S(2)}) async-start(bf16[1,32,4,16,2048]{4,3,2,0,1:T(8,128)(2,1)} %bitcast.76), calls=%async_computation.1 | async-start | bytes 16777216 | tf_op jit(solution)/shard_map/all_to_all | solution.py:40
  51.3 5.0 %multiply_convert_fusion.1 = bf16[512,2048]{1,0:T(8,128)(2,1)S(1)} fusion(bf16[512,1024]{1,0:T(8,128)(2,1)S(1)} %fusion.21, bf16[1024,2048]{1,0:T(8,128)(2,1)} %param.17), kind=kOutput, calls=%fused_computation.16 | convolution fusion | flops 2152726528 | bytes 7340032 | tf_op jit(solution)/shard_map/dot_general | solution.py:18
  56.3 1.4 copy-done.2
  57.8 177.9 %all-to-all-done.1 = bf16[1,32,4,16,2048]{4,3,2,0,1:T(8,128)(2,1)} async-done(((bf16[1,32,4,16,2048]{4,3,2,0,1:T(8,128)(2,1)}), bf16[1,32,4,16,2048]{4,3,2,0,1:T(8,128)(2,1)}, u32[]{:S(2)}, u32[]{:S(2)}) %all-to-all-start.1) | async-done | bytes 8388640 | tf_op jit(solution)/shard_map/all_to_all | solution.py:40
  235.7 58.1 %while.13 = (s32[]{:T(128)}, f32[8,512,128]{2,1,0:T(8,128)}, s32[8]{0:T(128)S(1)}, bf16[512,1024]{1,0:T(8,128)(2,1)S(1)}, bf16[2048,2048]{1,0:T(8,128)(2,1)}, /*...) while((s32[]{:T(128)}, f32[8,512,128]{2,1,0:T(8,128)}, ...), condition=%wide.region_8.9_spmd.clone, body=%wide.region_7.8_spmd.clone.sunk | while | flops 545265664 | bytes 1500472 | solution.py:95
  239.6 3.4 %fusion.47 = f32[8,512,128]{2,1,0:T(8,128)} fusion(f32[8,512,128]{2,1,0:T(8,128)} %get-tuple-element.196, s32[]{:T(128)} %get-tuple-element.195, f32[2048]{0:T(1024)S(1)} %reshape.139, f32[2048]{0:T(1024)S(1)} %bitcast.79, bf16[2048,2048]{1,0:T(8,128)(2,1)} %get-tuple-element.214, s32[]{:T(128)S(6)} %select_n.40, s32[]{:T(128)S(6)} %select_n.41, ...), kind=kOutput, calls=%fused_computation.6.clone.1 | convolution fusion | flops 545259520 | bytes 1458700 | tf_op jit(solution)/shard_map/while/body/eval_jaxpr/dot_general | solution.py:93
  246.9 3.4 %fusion.47 = f32[8,512,128]{2,1,0:T(8,128)} fusion(f32[8,512,128]{2,1,0:T(8,128)} %get-tuple-element.196, s32[]{:T(128)} %get-tuple-element.195, f32[2048]{0:T(1024)S(1)} %reshape.139, f32[2048]{0:T(1024)S(1)} %bitcast.79, bf16[2048,2048]{1,0:T(8,128)(2,1)} %get-tuple-element.214, s32[]{:T(128)S(6)} %select_n.40, s32[]{:T(128)S(6)} %select_n.41, ...), kind=kOutput, calls=%fused_computation.6.clone.1 | convolution fusion | flops 545259520 | bytes 1458700 | tf_op jit(solution)/shard_map/while/body/eval_jaxpr/dot_general | solution.py:93
  254.2 3.4 %fusion.47 = f32[8,512,128]{2,1,0:T(8,128)} fusion(f32[8,512,128]{2,1,0:T(8,128)} %get-tuple-element.196, s32[]{:T(128)} %get-tuple-element.195, f32[2048]{0:T(1024)S(1)} %reshape.139, f32[2048]{0:T(1024)S(1)} %bitcast.79, bf16[2048,2048]{1,0:T(8,128)(2,1)} %get-tuple-element.214, s32[]{:T(128)S(6)} %select_n.40, s32[]{:T(128)S(6)} %select_n.41, ...), kind=kOutput, calls=%fused_computation.6.clone.1 | convolution fusion | flops 545259520 | bytes 1458700 | tf_op jit(solution)/shard_map/while/body/eval_jaxpr/dot_general | solution.py:93
  261.5 3.4 %fusion.47 = f32[8,512,128]{2,1,0:T(8,128)} fusion(f32[8,512,128]{2,1,0:T(8,128)} %get-tuple-element.196, s32[]{:T(128)} %get-tuple-element.195, f32[2048]{0:T(1024)S(1)} %reshape.139, f32[2048]{0:T(1024)S(1)} %bitcast.79, bf16[2048,2048]{1,0:T(8,128)(2,1)} %get-tuple-element.214, s32[]{:T(128)S(6)} %select_n.40, s32[]{:T(128)S(6)} %select_n.41, ...), kind=kOutput, calls=%fused_computation.6.clone.1 | convolution fusion | flops 545259520 | bytes 1458700 | tf_op jit(solution)/shard_map/while/body/eval_jaxpr/dot_general | solution.py:93
  268.7 3.4 %fusion.47 = f32[8,512,128]{2,1,0:T(8,128)} fusion(f32[8,512,128]{2,1,0:T(8,128)} %get-tuple-element.196, s32[]{:T(128)} %get-tuple-element.195, f32[2048]{0:T(1024)S(1)} %reshape.139, f32[2048]{0:T(1024)S(1)} %bitcast.79, bf16[2048,2048]{1,0:T(8,128)(2,1)} %get-tuple-element.214, s32[]{:T(128)S(6)} %select_n.40, s32[]{:T(128)S(6)} %select_n.41, ...), kind=kOutput, calls=%fused_computation.6.clone.1 | convolution fusion | flops 545259520 | bytes 1458700 | tf_op jit(solution)/shard_map/while/body/eval_jaxpr/dot_general | solution.py:93
  276.0 3.4 %fusion.47 = f32[8,512,128]{2,1,0:T(8,128)} fusion(f32[8,512,128]{2,1,0:T(8,128)} %get-tuple-element.196, s32[]{:T(128)} %get-tuple-element.195, f32[2048]{0:T(1024)S(1)} %reshape.139, f32[2048]{0:T(1024)S(1)} %bitcast.79, bf16[2048,2048]{1,0:T(8,128)(2,1)} %get-tuple-element.214, s32[]{:T(128)S(6)} %select_n.40, s32[]{:T(128)S(6)} %select_n.41, ...), kind=kOutput, calls=%fused_computation.6.clone.1 | convolution fusion | flops 545259520 | bytes 1458700 | tf_op jit(solution)/shard_map/while/body/eval_jaxpr/dot_general | solution.py:93
  283.2 3.4 %fusion.47 = f32[8,512,128]{2,1,0:T(8,128)} fusion(f32[8,512,128]{2,1,0:T(8,128)} %get-tuple-element.196, s32[]{:T(128)} %get-tuple-element.195, f32[2048]{0:T(1024)S(1)} %reshape.139, f32[2048]{0:T(1024)S(1)} %bitcast.79, bf16[2048,2048]{1,0:T(8,128)(2,1)} %get-tuple-element.214, s32[]{:T(128)S(6)} %select_n.40, s32[]{:T(128)S(6)} %select_n.41, ...), kind=kOutput, calls=%fused_computation.6.clone.1 | convolution fusion | flops 545259520 | bytes 1458700 | tf_op jit(solution)/shard_map/while/body/eval_jaxpr/dot_general | solution.py:93
  290.5 3.4 %fusion.47 = f32[8,512,128]{2,1,0:T(8,128)} fusion(f32[8,512,128]{2,1,0:T(8,128)} %get-tuple-element.196, s32[]{:T(128)} %get-tuple-element.195, f32[2048]{0:T(1024)S(1)} %reshape.139, f32[2048]{0:T(1024)S(1)} %bitcast.79, bf16[2048,2048]{1,0:T(8,128)(2,1)} %get-tuple-element.214, s32[]{:T(128)S(6)} %select_n.40, s32[]{:T(128)S(6)} %select_n.41, ...), kind=kOutput, calls=%fused_computation.6.clone.1 | convolution fusion | flops 545259520 | bytes 1458700 | tf_op jit(solution)/shard_map/while/body/eval_jaxpr/dot_general | solution.py:93
  293.9 1.8 reduce_sum.61
  295.7 2.1 fusion.19
  297.9 3.6 %convolution_convert_fusion = bf16[512,1024]{1,0:T(8,128)(2,1)} fusion(bf16[1024,1024]{1,0:T(8,128)(2,1)S(1)} %copy-done, bf16[512,2048]{1,0:T(8,128)(2,1)} %copy-done.2, f32[512]{0:T(512)S(1)} %add_rsqrt_fusion.1, f32[512]{0:T(512)S(1)} %broadcast_multiply_fusion.1, f32[8,512,128]{2,1,0:T(8,128)S(1)} %copy-done.1), kind=kOutput, calls=%fused_computation.29 | convolution fusion | flops 1076887552 | bytes 6295552 | tf_op jit(solution)/shard_map/dot_general | solution.py:99
  301.4 3.7 %all-to-all-start.3 = ((bf16[32,16,1024]{2,1,0:T(8,128)(2,1)}), bf16[32,16,1024]{2,1,0:T(8,128)(2,1)S(1)}, u32[]{:S(2)}, u32[]{:S(2)}) async-start(bf16[32,16,1024]{2,1,0:T(8,128)(2,1)} %bitcast.78), calls=%async_computation.3 | async-start | bytes 2097152 | tf_op jit(solution)/shard_map/all_to_all | solution.py:24
  305.2 24.7 %all-to-all-done.3 = bf16[32,16,1024]{2,1,0:T(8,128)(2,1)S(1)} async-done(((bf16[32,16,1024]{2,1,0:T(8,128)(2,1)}), bf16[32,16,1024]{2,1,0:T(8,128)(2,1)S(1)}, u32[]{:S(2)}, u32[]{:S(2)}) %all-to-all-start.3) | async-done | bytes 1048608 | tf_op jit(solution)/shard_map/all_to_all | solution.py:24
  329.9 2.0 gather_fusion
  331.8 2.2 add_convert_fusion
  (66 shorter events, 16.4 us)
Async XLA Ops:
  0.0 297.8 %copy-start = (bf16[1024,1024]{1,0:T(8,128)(2,1)S(1)}, bf16[1024,1024]{1,0:T(8,128)(2,1)}, u32[]{:S(2)}) copy-start(bf16[1024,1024]{1,0:T(8,128)(2,1)} %param.18) | copy-start | bytes 6291460
  1.6 12.5 %all-to-all-start.2 = ((s32[1,32,4,16]{3,2,0,1:T(4,128)}), s32[1,32,4,16]{3,2,0,1:T(4,128)S(1)}, u32[]{:S(2)}, u32[]{:S(2)}) async-start(s32[1,32,4,16]{3,2,0,1:T(4,128)} %copy.20), calls=%async_computation.2 | async-start | bytes 131072 | tf_op jit(solution)/shard_map/all_to_all | solution.py:41
  44.7 4.9 %copy-start.4 = (s32[1,128]{1,0:T(1,128)S(1)}, s32[1,128]{1,0:T(1,128)}, u32[]{:S(2)}) copy-start(s32[1,128]{1,0:T(1,128)} %param.14) | copy-start | bytes 1540
  44.7 5.1 %copy-start.3 = (f32[8,128]{1,0:T(8,128)S(1)}, f32[8,128]{1,0:T(8,128)}, u32[]{:S(2)}) copy-start(f32[8,128]{1,0:T(8,128)} %param.19) | copy-start | bytes 12292
  44.7 191.1 %all-to-all-start.1 = ((bf16[1,32,4,16,2048]{4,3,2,0,1:T(8,128)(2,1)}), bf16[1,32,4,16,2048]{4,3,2,0,1:T(8,128)(2,1)}, u32[]{:S(2)}, u32[]{:S(2)}) async-start(bf16[1,32,4,16,2048]{4,3,2,0,1:T(8,128)(2,1)} %bitcast.76), calls=%async_computation.1 | async-start | bytes 16777216 | tf_op jit(solution)/shard_map/all_to_all | solution.py:40
  56.3 1.4 copy-start.2
  295.6 2.2 copy-start.1
  301.4 28.4 %all-to-all-start.3 = ((bf16[32,16,1024]{2,1,0:T(8,128)(2,1)}), bf16[32,16,1024]{2,1,0:T(8,128)(2,1)S(1)}, u32[]{:S(2)}, u32[]{:S(2)}) async-start(bf16[32,16,1024]{2,1,0:T(8,128)(2,1)} %bitcast.78), calls=%async_computation.3 | async-start | bytes 2097152 | tf_op jit(solution)/shard_map/all_to_all | solution.py:24
where the time goes:
time: 338 us; the launch traced here: 334 us
  waiting for transfers between devices  203 us (60%)
  matrix products  36 us (11%)
  blocking collectives  30.5 us (9%)
  loops' own time  19.7 us (6%)
  other arithmetic  15.7 us (5%)
  starting transfers between devices  14.9 us (4%)
  local copies, waits for them, and re-layouts  14.4 us (4%)
    all_to_all x1, waiting for transfers between devices, shards(): lax.all_to_all(kv_store, ('req', 'cache'), split_axis=1, concat_axis=0, t...  178 us
    all_to_all x1, blocking collectives, shards(): lax.all_to_all(empty.at[flat_slot].set(cand_x).reshape(devices, capacity,...  30.5 us
    dot_general x8, matrix products, one_head(): return jnp.dot(weight, value_head, preferred_element_type=jnp.float32)  27 us
    all_to_all x1, waiting for transfers between devices, send_back(): lax.all_to_all(update, ('req', 'cache'), split_axis=0, concat_axis=0, til...  24.7 us
    another operation x1, loops' own time, shards(): per_head = lax.map(one_head, jnp.arange(head_count, dtype=jnp.int32))  19.7 us
  transfers between devices with their start and end apart: 3, of which 2 were waited for; matrix products, arithmetic and copies ran while one was open for 4% of the time, Pallas kernels for 0%

commit v1 on v0

--- a/solution.py
+++ b/solution.py
@@ -1,8 +1,11 @@
+import functools
 import math
 
 import jax
 import jax.numpy as jnp
 from jax import lax
+from jax.experimental import pallas as pl
+from jax.experimental.pallas import tpu as pltpu
 from jax.sharding import PartitionSpec as P
 
 
@@ -18,6 +21,12 @@
     return jax.nn.silu(jnp.dot(normed, w_proj, preferred_element_type=jnp.float32)).astype(
         jnp.bfloat16
     )
+
+
+def rank_of(target):
+    index = jnp.arange(target.shape[0], dtype=jnp.int32)
+    same = (target[:, None] == target[None, :]) & (index[None, :] < index[:, None])
+    return jnp.sum(same.astype(jnp.int32), axis=1)
 
 
 def send_back(update):
@@ -58,10 +67,7 @@
     bias = jnp.dot(time_bias, bucket_table, precision=lax.Precision.HIGHEST)
     score_scale = 1.0 / math.sqrt(head_dim)
     target = cand_req[:, 0]
-    onehot = (target[:, None] == jnp.arange(devices, dtype=jnp.int32)[None, :]).astype(jnp.int32)
-    earlier = jnp.cumsum(onehot, axis=0) - onehot
-    slot_rank = jnp.sum(earlier * onehot, axis=1)
-    flat_slot = target * capacity + slot_rank
+    flat_slot = target * capacity + rank_of(target)
     empty = jnp.zeros((devices * capacity, cand_x.shape[1]), cand_x.dtype)
     received = lax.all_to_all(
         empty.at[flat_slot].set(cand_x).reshape(devices, capacity, cand_x.shape[1]),
@@ -105,6 +111,452 @@
     return (cand_x.astype(jnp.float32) + update.astype(jnp.float32)).astype(jnp.bfloat16)
 
 
+MESH = pl.DeviceIdType.MESH
+ANY = pl.BlockSpec(memory_space=pl.ANY)
+VMEM = pl.BlockSpec(memory_space=pltpu.VMEM)
+
+
+def place():
+    req, z = lax.axis_index("req"), lax.axis_index("cache")
+    core = lax.rem(req, 2)
+    x = lax.rem(req // 2, 2)
+    y = req // 4
+    return req, z, core, x, y
+
+
+def greet(others):
+    barrier = pltpu.get_barrier_semaphore()
+    for other in others:
+        pl.semaphore_signal(barrier, inc=1, device_id=other, device_id_type=MESH)
+    pl.semaphore_wait(barrier, len(others))
+
+
+def remote(src, dst, send, recv, device):
+    return pltpu.make_async_remote_copy(
+        src_ref=src,
+        dst_ref=dst,
+        send_sem=send,
+        recv_sem=recv,
+        device_id=device,
+        device_id_type=MESH,
+    )
+
+
+def spread_kernel(
+    q_ref, kv_ref, meta_ref, bucket_ref, qall, kvp, meta_all, bucket_p,
+    local_sem, pair_send, pair_recv, meta_send, meta_recv,
+    z_send, z_recv, a_send, a_recv, e_send, e_recv, f_send, f_recv,
+):
+    req, z, core, x, y = place()
+    partner = (req + 1 - 2 * core, z)
+    xn = (y * 4 + (1 - x) * 2 + core, z)
+    yn = ((1 - y) * 4 + x * 2 + core, z)
+    rows = q_ref.shape[0]
+    half = q_ref.shape[1] // 2
+    reqs, zs = lax.axis_size("req"), lax.axis_size("cache")
+    others = []
+    for step in range(1, reqs * zs):
+        others.append((lax.rem(req + step // zs, reqs), lax.rem(z + step % zs, zs)))
+    greet(others)
+
+    def slot(zz, yy, xx):
+        return (zz * 2 + yy) * 2 + xx
+
+    mine = slot(z, y, x)
+    my_cols = pl.ds(pl.multiple_of(core * half, half), half)
+    other_start = pl.multiple_of((1 - core) * half, half)
+    other_cols = pl.ds(other_start, half)
+    other_values = pl.ds(pl.multiple_of(2 * half + (1 - core) * half, half), half)
+    my_rows = pl.ds(pl.multiple_of(core * rows, rows), rows)
+    pair = [
+        remote(q_ref.at[:, other_cols], qall.at[mine, my_rows, :], pair_send.at[0], pair_recv.at[0], partner),
+        remote(kv_ref.at[:, other_cols], kvp.at[0], pair_send.at[1], pair_recv.at[1], partner),
+        remote(kv_ref.at[:, other_values], kvp.at[1], pair_send.at[2], pair_recv.at[2], partner),
+        remote(bucket_ref, bucket_p, pair_send.at[3], pair_recv.at[3], partner),
+    ]
+    pair[0].start()
+    own = pltpu.make_async_copy(q_ref.at[:, my_cols], qall.at[mine, my_rows, :], local_sem.at[0])
+    own.start()
+    own_meta = pltpu.make_async_copy(meta_ref, meta_all.at[req * zs + z], local_sem.at[1])
+    own_meta.start()
+    metas = []
+    for step, other in enumerate(others):
+        copy = remote(
+            meta_ref, meta_all.at[req * zs + z], meta_send.at[step], meta_recv.at[step], other
+        )
+        metas.append(copy)
+    own.wait()
+    pair[0].wait_recv()
+
+    first, second = pl.ds(0, rows), pl.ds(rows, rows)
+    started = []
+
+    def go(ref, send, recv, device):
+        copy = remote(ref, ref, send, recv, device)
+        copy.start()
+        started.append(copy)
+        return copy
+
+    z_copies = [None]
+    for j in range(1, zs):
+        z_copies.append(go(qall.at[mine], z_send.at[j], z_recv.at[j], (req, lax.rem(z + j, zs))))
+    hops = []
+    forwards = []
+    for j in range(zs + 1):
+        if j < zs:
+            zz = lax.rem(z - j + zs, zs)
+            if j > 0:
+                z_copies[j].wait_recv()
+            here = slot(zz, y, x)
+            hops.append((
+                go(qall.at[here, first, :], a_send.at[0, j], a_recv.at[0, j], yn),
+                go(qall.at[here, second, :], a_send.at[1, j], a_recv.at[1, j], xn),
+            ))
+            forwards.append(
+                go(qall.at[here, first, :], e_send.at[0, j], e_recv.at[0, j], xn)
+            )
+            forwards.append(
+                go(qall.at[here, second, :], e_send.at[1, j], e_recv.at[1, j], yn)
+            )
+        if j == 0:
+            for copy in metas:
+                copy.start()
+            for copy in pair[1:]:
+                copy.start()
+        if j > 0:
+            i = j - 1
+            zz = lax.rem(z - i + zs, zs)
+            hops[i][0].wait_recv()
+            forwards.append(
+                go(qall.at[slot(zz, 1 - y, x), first, :], f_send.at[0, i], f_recv.at[0, i], xn)
+            )
+            hops[i][1].wait_recv()
+            forwards.append(
+                go(qall.at[slot(zz, y, 1 - x), second, :], f_send.at[1, i], f_recv.at[1, i], yn)
+            )
+    for copy in forwards:
+        copy.wait_recv()
+    for copy in started:
+        copy.wait_send()
+    for copy in metas:
+        copy.wait()
+    own_meta.wait()
+    pair[0].wait_send()
+    for copy in pair[1:]:
+        copy.wait()
+
+
+def spread(query, kv, meta, buckets):
+    rows, features = query.shape
+    events = kv.shape[0]
+    reqs, zs = lax.axis_size("req"), lax.axis_size("cache")
+    devices = reqs * zs
+    dma = pltpu.SemaphoreType.DMA
+    return pl.pallas_call(
+        spread_kernel,
+        out_shape=(
+            jax.ShapeDtypeStruct((devices // 2, 2 * rows, features // 2), query.dtype),
+            jax.ShapeDtypeStruct((2, events, features // 2), kv.dtype),
+            jax.ShapeDtypeStruct((devices,) + meta.shape, meta.dtype),
+            jax.ShapeDtypeStruct(buckets.shape, buckets.dtype),
+        ),
+        in_specs=[ANY] * 4,
+        out_specs=(ANY,) * 4,
+        scratch_shapes=[
+            dma((2,)), dma((4,)), dma((4,)), dma((devices - 1,)), dma((devices - 1,)),
+            dma((zs,)), dma((zs,)), dma((2, zs)), dma((2, zs)), dma((2, zs)), dma((2, zs)),
+            dma((2, zs)), dma((2, zs)),
+        ],
+        compiler_params=pltpu.CompilerParams(collective_id=0, has_side_effects=True),
+    )(query, kv, meta, buckets)
+
+
+def attend_kernel(scale, q_ref, slot_ref, k_ref, v_ref, bias_ref, live_ref, out_ref, slots):
+    chips, chip_rows, cols = q_ref.shape
+    requests, slot_rows, _ = slots.shape
+    devices = slot_ref.shape[0]
+    rows = chip_rows // 2
+    cap = slot_rows // devices
+
+    def chosen(d):
+        ids = lax.broadcasted_iota(jnp.int32, (requests * cap, rows), 0)
+        return jnp.where(ids == slot_ref[d], 1.0, 0.0).astype(jnp.bfloat16)
+
+    @pl.loop(0, chips)
+    def _(chip):
+        for part in range(2):
+            got = jnp.dot(
+                chosen(chip * 2 + part),
+                q_ref[chip, part * rows : (part + 1) * rows, :],
+                preferred_element_type=jnp.float32,
+            ).astype(jnp.bfloat16)
+            start = pl.multiple_of((chip * 2 + part) * cap, cap)
+            slots[:, pl.ds(start, cap), :] = got.reshape(requests, cap, cols)
+
+    pair = 256
+    count = k_ref.shape[1]
+    zero = jnp.zeros((count, pair // 2), jnp.bfloat16)
+
+    @pl.loop(0, requests)
+    def _(q):
+        for hp in range(cols // pair):
+            span = slice(hp * pair, (hp + 1) * pair)
+
+            def diagonal(block):
+                return jnp.concatenate(
+                    [
+                        jnp.concatenate([block[:, : pair // 2], zero], axis=1),
+                        jnp.concatenate([zero, block[:, pair // 2 :]], axis=1),
+                    ],
+                    axis=0,
+                )
+
+            scores = lax.dot_general(
+                slots[q, :, span],
+                diagonal(k_ref[q, :, span]),
+                (((1,), (1,)), ((), ())),
+                preferred_element_type=jnp.float32,
+            )
+            halved = scores * (0.5 * scale) + bias_ref[q, hp : hp + 1, :]
+            weight = (halved + halved * jnp.tanh(halved)) * live_ref[q]
+            slots[q, :, span] = jnp.dot(
+                weight.astype(jnp.bfloat16),
+                diagonal(v_ref[q, :, span]),
+                preferred_element_type=jnp.float32,
+            ).astype(jnp.bfloat16)
+
+    @pl.loop(0, chips)
+    def _(chip):
+        for part in range(2):
+            start = pl.multiple_of((chip * 2 + part) * cap, cap)
+            block = slots[:, pl.ds(start, cap), :].reshape(requests * cap, cols)
+            out_ref[chip, part * rows : (part + 1) * rows, :] = lax.dot_general(
+                chosen(chip * 2 + part),
+                block,
+                (((0,), (0,)), ((), ())),
+                preferred_element_type=jnp.float32,
+            ).astype(jnp.bfloat16)
+
+
+def attend(qall, slot_rows, keys, values, bias, live, scale, requests, cap):
+    devices = slot_rows.shape[0]
+    cols = qall.shape[2]
+    return pl.pallas_call(
+        functools.partial(attend_kernel, scale),
+        out_shape=jax.ShapeDtypeStruct(qall.shape, jnp.bfloat16),
+        in_specs=[VMEM] * 6,
+        out_specs=VMEM,
+        scratch_shapes=[pltpu.VMEM((requests, devices * cap, cols), jnp.bfloat16)],
+        compiler_params=pltpu.CompilerParams(vmem_limit_bytes=58 * 2**20),
+        cost_estimate=pl.CostEstimate(
+            flops=2 * 10**10, bytes_accessed=24 * 2**20, transcendentals=8 * 10**6
+        ),
+    )(qall, slot_rows, keys, values, bias, live)
+
+
+def collect_kernel(
+    part, mine_out, theirs_out, got1, got2, sum1, sum2, got_z, total,
+    s1, r1, s2, r2, sz, rz, sp, rp,
+):
+    req, z, core, x, y = place()
+    partner = (req + 1 - 2 * core, z)
+    xn = (y * 4 + (1 - x) * 2 + core, z)
+    yn = ((1 - y) * 4 + x * 2 + core, z)
+    zs = lax.axis_size("cache")
+    rows = part.shape[1] // 2
+    f32 = jnp.float32
+    greet([partner, xn, yn] + [(req, lax.rem(z + j, zs)) for j in range(1, zs)])
+
+    def slot(zz, yy, xx):
+        return (zz * 2 + yy) * 2 + xx
+
+    spans = (slice(0, rows), slice(rows, 2 * rows))
+    windows = (pl.ds(0, rows), pl.ds(rows, rows))
+    order = list(range(1, zs)) + [0]
+    firsts, seconds, z_copies = {}, {}, {}
+    for j in order:
+        zz = lax.rem(z + j, zs)
+        for k in range(2):
+            for keep in (0, 1):
+                for h in range(2):
+                    if h == 0:
+                        source = slot(zz, (y if keep else 1 - y), 1 - x)
+                        target = xn
+                    else:
+                        source = slot(zz, 1 - y, (x if keep else 1 - x))
+                        target = yn
+                    if keep != k:
+                        continue
+                    copy = remote(
+                        part.at[source, windows[h], :],
+                        got1.at[j, h, keep],
+                        s1.at[j, h, keep],
+                        r1.at[j, h, keep],
+                        target,
+                    )
+                    copy.start()
+                    firsts[j, h, keep] = copy
+    for step in range(len(order) + 1):
+        if step < len(order):
+            j = order[step]
+            zz = lax.rem(z + j, zs)
+            for h in range(2):
+                firsts[j, h, 0].wait_recv()
+                away = slot(zz, 1 - y, x) if h == 0 else slot(zz, y, 1 - x)
+                sum1[j, h] = (
+                    part[away, spans[h], :].astype(f32) + got1[j, h, 0].astype(f32)
+                ).astype(jnp.bfloat16)
+                copy = remote(
+                    sum1.at[j, h], got2.at[j, h], s2.at[j, h], r2.at[j, h], yn if h == 0 else xn
+                )
+                copy.start()
+                seconds[j, h] = copy
+        if step > 0:
+            j = order[step - 1]
+            zz = lax.rem(z + j, zs)
+            for h in range(2):
+                firsts[j, h, 1].wait_recv()
+                seconds[j, h].wait_recv()
+                here = (
+                    part[slot(zz, y, x), spans[h], :].astype(f32)
+                    + got1[j, h, 1].astype(f32)
+                    + got2[j, h].astype(f32)
+                )
+                if j == 0:
+                    total[h] = here
+                else:
+                    sum2[j, h] = here.astype(jnp.bfloat16)
+                    copy = remote(
+                        sum2.at[j, h], got_z.at[j, h], sz.at[j, h], rz.at[j, h], (req, zz)
+                    )
+                    copy.start()
+                    z_copies[j, h] = copy
+    for h in range(2):
+        for j in range(1, zs):
+            z_copies[j, h].wait_recv()
+            total[h] = total[h] + got_z[j, h].astype(f32)
+    swap = remote(total.at[1 - core], theirs_out, sp.at[0], rp.at[0], partner)
+    swap.start()
+    mine_out[...] = total[core]
+    for copies in (firsts, seconds, z_copies):
+        for copy in copies.values():
+            copy.wait_send()
+    swap.wait()
+
+
+def collect(part):
+    rows, cols = part.shape[1] // 2, part.shape[2]
+    zs = lax.axis_size("cache")
+    dma = pltpu.SemaphoreType.DMA
+    b16 = jnp.bfloat16
+    return pl.pallas_call(
+        collect_kernel,
+        out_shape=(jax.ShapeDtypeStruct((rows, cols), jnp.float32),) * 2,
+        in_specs=[VMEM],
+        out_specs=(VMEM, VMEM),
+        scratch_shapes=[
+            pltpu.VMEM((zs, 2, 2, rows, cols), b16),
+            pltpu.VMEM((zs, 2, rows, cols), b16),
+            pltpu.VMEM((zs, 2, rows, cols), b16),
+            pltpu.VMEM((zs, 2, rows, cols), b16),
+            pltpu.VMEM((zs, 2, rows, cols), b16),
+            pltpu.VMEM((2, rows, cols), jnp.float32),
+            dma((zs, 2, 2)), dma((zs, 2, 2)), dma((zs, 2)), dma((zs, 2)),
+            dma((zs, 2)), dma((zs, 2)), dma((1,)), dma((1,)),
+        ],
+        compiler_params=pltpu.CompilerParams(
+            collective_id=1, has_side_effects=True, vmem_limit_bytes=48 * 2**20
+        ),
+    )(part)
+
+
+def gathered(
+    cand_x, cand_req, hist_len, block_place, kv_store, store_bucket, w_proj, w_out, time_bias
+):
+    reqs, zs = lax.axis_size("req"), lax.axis_size("cache")
+    devices = reqs * zs
+    rows, features = cand_x.shape
+    heads, bucket_count = time_bias.shape
+    half_heads = heads // 2
+    per_owner, block_ev = kv_store.shape[2], kv_store.shape[3]
+    own_events = per_owner * block_ev
+    requests = kv_store.shape[1]
+    cap = max(2, 2 * rows // devices)
+    req, z, core, _, _ = place()
+
+    places = block_place[0]
+    blocks = places.shape[0]
+    ids = jnp.arange(blocks, dtype=jnp.int32)
+    match = (places[:, None] == ids[None, :]).astype(jnp.int32)
+    block_of_place = jnp.sum(match * ids[:, None], axis=0)
+    alive = jnp.clip(hist_len[0] - block_of_place * block_ev, 0, block_ev)
+    target = cand_req[:, 0]
+    flat_slot = target * cap + rank_of(target)
+    meta = jnp.concatenate(
+        [alive, flat_slot, jnp.zeros((8 * 128 - blocks - rows,), jnp.int32)]
+    ).reshape(8, 128)
+
+    projected = prepare(cand_x, w_proj)
+    gate_u = projected[:, :features]
+    query = projected[:, features:]
+    kv = kv_store.reshape(requests * own_events, 2 * features)
+    qall, kvp, meta_all, bucket_p = spread(
+        query, kv, meta, store_bucket.reshape(requests * own_events // 128, 128)
+    )
+
+    half = features // 2
+    info = meta_all.reshape(devices, 8 * 128)
+    slot_rows = info[:, blocks : blocks + rows].reshape(2, 2, 2, zs, rows)
+    slot_rows = jnp.transpose(slot_rows, (3, 0, 1, 2, 4)).reshape(devices, 1, rows)
+    alive_all = info[:, :blocks].reshape(devices, devices // 2 * 2, per_owner)
+    me = req * zs + z
+    other = (req + 1 - 2 * core) * zs + z
+    event = jnp.arange(block_ev, dtype=jnp.int32)
+
+    def live_of(owner):
+        counts = lax.dynamic_slice_in_dim(alive_all, owner, 1, 1)[:, 0, :]
+        return (event[None, None, :] < counts[:, :, None]).reshape(devices, own_events)
+
+    live = jnp.concatenate([live_of(me), live_of(other)], axis=1).astype(jnp.float32)
+    buckets = jnp.concatenate(
+        [store_bucket.reshape(requests, own_events), bucket_p.reshape(requests, own_events)], axis=1
+    )
+    events = 2 * own_events
+    table = (
+        buckets.reshape(1, requests * events)
+        == jnp.arange(bucket_count, dtype=jnp.int32)[:, None]
+    ).astype(jnp.float32)
+    my_bias = lax.dynamic_slice_in_dim(time_bias, core * half_heads, half_heads, 0)
+    bias = 0.5 * jnp.dot(my_bias, table, precision=lax.Precision.HIGHEST)
+    bias = jnp.transpose(bias.reshape(half_heads, requests, events), (1, 0, 2))
+    bias = bias.reshape(requests, half_heads // 2, 2 * events)
+    live = jnp.concatenate([live, live], axis=1).reshape(requests, 1, 2 * events)
+
+    def joined(start, received):
+        mine = lax.dynamic_slice_in_dim(kv, start + core * half, half, 1)
+        return jnp.concatenate(
+            [
+                mine.reshape(requests, own_events, half),
+                received.reshape(requests, own_events, half),
+            ],
+            axis=1,
+        )
+
+    part = attend(
+        qall, slot_rows, joined(0, kvp[0]), joined(features, kvp[1]), bias, live,
+        1.0 / math.sqrt(features // heads), requests, cap,
+    )
+    mine, theirs = collect(part)
+    attended = jnp.where(
+        core == 0,
+        jnp.concatenate([mine, theirs], axis=1),
+        jnp.concatenate([theirs, mine], axis=1),
+    )
+    hidden = (layer_norm(attended) * gate_u.astype(jnp.float32)).astype(jnp.bfloat16)
+    update = jnp.dot(hidden, w_out, preferred_element_type=jnp.float32).astype(jnp.bfloat16)
+    return (cand_x.astype(jnp.float32) + update.astype(jnp.float32)).astype(jnp.bfloat16)
+
+
 def solution(mesh):
     placed = (
         P(("req", "cache"), None),
@@ -117,6 +569,7 @@
         P(),
         P(),
     )
+    body = gathered if mesh.shape["req"] == 8 and mesh.shape["cache"] == 4 else shards
     return jax.shard_map(
-        shards, mesh=mesh, in_specs=placed, out_specs=P(("req", "cache"), None), check_vma=False
-    )
+        body, mesh=mesh, in_specs=placed, out_specs=P(("req", "cache"), None), check_vma=False
+    )

time: 338 us -> 290 us (0.86); the launches traced: 334 us -> 290 us
  Pallas kernels: 0 us -> 257 us
  waiting for transfers between devices: 203 us -> 0 us
  blocking collectives: 30.5 us -> 0 us
  matrix products: 36 us -> 6.12 us
  loops' own time: 19.7 us -> 0 us
  starting transfers between devices: 14.9 us -> 0 us
  other arithmetic: 15.7 us -> 9.8 us
    pallas_call x0 -> x3, Pallas kernels: none -> 257 us  [the longest x1 123 us: collect(): pl.pallas_call(collect_kernel, out_shape=(jax.ShapeDtypeStruct((rows, col...]
    all_to_all x3 -> x0, waiting for transfers between devices: 203 us -> none  [the longest x1 178 us: shards(): lax.all_to_all(kv_store, ('req', 'cache'), split_axis=1, concat_axis=0, t...]
    all_to_all x1 -> x0, blocking collectives: 30.5 us -> none  [shards(): lax.all_to_all(empty.at[flat_slot].set(cand_x).reshape(devices, capacity,...]
    dot_general x10 -> x2, matrix products: 31 us -> 2.32 us  [the longest x1 1.57 us: gathered(): jnp.dot(hidden, w_out, preferred_element_type=jnp.float32)]
    another operation x1 -> x0, loops' own time: 19.7 us -> none  [shards(): per_head = lax.map(one_head, jnp.arange(head_count, dtype=jnp.int32))]
    all_to_all x3 -> x0, starting transfers between devices: 14.9 us -> none  [the longest x1 6.36 us: shards(): lax.all_to_all(store_bucket, ('req', 'cache'), split_axis=1, concat_axis=...]
    convert_element_type x11 -> x0, other arithmetic: 9 us -> none  [the longest x8 5.81 us: shards(): live = (position < hist_len[0]).astype(jnp.float32)]
    reshape x0 -> x7, local copies, waits for them, and re-layouts: none -> 4.3 us  [the longest x1 0.82 us: gathered(): store_bucket.reshape(requests, own_events)]
  transfers between devices with their start and end apart: 3 -> 0, of which waited for: 2 -> 0; matrix products, arithmetic and copies ran while one was open for 4% -> 0% of each run, Pallas kernels for 0% -> 0%
where the time goes in v1:
time: 290 us
  Pallas kernels  257 us (89%)
  local copies, waits for them, and re-layouts  15.8 us (5%)
  other arithmetic  9.8 us (3%)
  matrix products  6.12 us (2%)
    pallas_call x1, Pallas kernels, collect(): pl.pallas_call(collect_kernel, out_shape=(jax.ShapeDtypeStruct((rows, col...  123 us
    pallas_call x1, Pallas kernels, spread(): pl.pallas_call(spread_kernel, out_shape=(jax.ShapeDtypeStruct((devices //...  87.3 us
    pallas_call x1, Pallas kernels, attend(): pl.pallas_call(functools.partial(attend_kernel, scale), out_shape=jax.Sha...  46.5 us

profile of v1, /device:TPU:9, one launch (start us, length us, event | category | flops | bytes accessed | tf_op | source)
XLA Modules:
  0.0 289.9 jit_solution(14116836441778404346)
XLA Ops:
  0.8 0.8 select_reduce_fusion
  1.6 0.9 convert_reduce_fusion.1
  2.5 0.7 multiply_add_fusion
  3.2 1.2 convert_reduce_fusion
  4.4 1.3 fusion.5
  6.4 0.8 copy.25
  7.2 0.9 copy.23
  8.1 0.7 reshape.82.bucket_ref
  8.8 3.8 %multiply_convert_fusion = bf16[256,2048]{1,0:T(8,128)(2,1)S(1)} fusion(bf16[1024,2048]{1,0:T(8,128)(2,1)} %param.15, bf16[256,1024]{1,0:T(8,128)(2,1)} %param.9, f32[256]{0:T(256)S(1)} %add_rsqrt_fusion.1, f32[256]{0:T(256)S(1)} %broadcast_multiply_fusion.1), kind=kOutput, calls=%fused_computation.4 | convolution fusion | flops 1077411840 | bytes 5769216 | tf_op jit(solution)/shard_map/dot_general | solution.py:21
  12.6 0.8 slice.24.q_ref
  13.4 4.5 %constant_dynamic-slice_fusion = (bf16[2048,512]{1,0:T(8,128)(2,1)}, bf16[2048,512]{1,0:T(8,128)(2,1)}) fusion(bf16[2048,2048]{1,0:T(8,128)(2,1)} %bitcast.32, s32[]{:T(128)S(6)} %select_n.25, s32[]{:T(128)S(6)} %select_n.24), kind=kLoop, calls=%fused_computation.42 | loop fusion | bytes 8388616 | tf_op jit(solution)/shard_map/dynamic_slice | solution.py:536
  17.9 87.3 %shard_map.91 = (bf16[16,512,512]{2,1,0:T(8,128)(2,1)}, bf16[2,2048,512]{2,1,0:T(8,128)(2,1)}, s32[32,8,128]{2,1,0:T(8,128)}, s32[16,128]{1,0:T(8,128)}) custom-call(bf16[256,1024]{1,0:T(8,128)(2,1)} %slice.24.q_ref, bf16[2048,2048]{1,0:T(8,128)(2,1)} %bitcast.33, s32[8,128]{1,0:T(8,128)} %add_bitcast_fusion.1.meta_ref, s32[16,128]{1,0:T(8,128)} %reshape.82.bucket_ref), custom_call_target="tpu_custom_call" | custom-call | tf_op jit(solution)/shard_map/pallas_call | solution.py:255
  105.2 0.9 copy.32
  106.2 0.7 reshape.85.slot_ref
  106.9 0.8 reshape.89
  107.7 0.8 fusion.4
  108.5 0.7 reshape.91.bias_ref
  109.5 0.7 reshape.96.live_ref
  110.2 2.7 fusion.22
  113.0 0.6 copy-done.2
  113.7 3.7 %pad_maximum_fusion = (bf16[32,128,512]{2,1,0:T(8,128)(2,1)}, bf16[32,128,512]{2,1,0:T(8,128)(2,1)}) fusion(bf16[32,64,512]{2,1,0:T(8,128)(2,1)S(1)} %bitcast.37, bf16[32,64,512]{2,1,0:T(8,128)(2,1)S(1)} %bitcast.35, bf16[32,64,512]{2,1,0:T(8,128)(2,1)S(1)} %bitcast.36, bf16[32,64,512]{2,1,0:T(8,128)(2,1)S(1)} %bitcast.34), kind=kLoop, calls=%fused_computation.1 | loop fusion | flops 16777216 | bytes 16777216 | tf_op jit(solution)/shard_map/concatenate | solution.py:537
  117.4 46.5 %shard_map.92.part = bf16[16,512,512]{2,1,0:T(8,128)(2,1)} custom-call(bf16[16,512,512]{2,1,0:T(8,128)(2,1)} %get-tuple-element.11.q_ref, s32[32,1,256]{2,1,0:T(1,128)} %reshape.85.slot_ref, bf16[32,128,512]{2,1,0:T(8,128)(2,1)} %get-tuple-element.25.k_ref, bf16[32,128,512]{2,1,0:T(8,128)(2,1)} %get-tuple-element.26.v_ref, f32[32,2,256]{2,1,0:T(2,128)} %reshape.91.bias_ref, ...), custom_call_target="tpu_custom_call" | custom-call | flops 20000000000 | bytes 25165824 | tf_op jit(solution)/shard_map/pallas_call | solution.py:344
  163.9 123.4 %shard_map.93 = (f32[256,512]{1,0:T(8,128)S(1)}, f32[256,512]{1,0:T(8,128)S(1)}) custom-call(bf16[16,512,512]{2,1,0:T(8,128)(2,1)} %shard_map.92.part), custom_call_target="tpu_custom_call" | custom-call | tf_op jit(solution)/shard_map/pallas_call | solution.py:452
  288.3 1.6 fusion.1
  (33 shorter events, 2.4 us)
Async XLA Ops:
  0.0 287.7 %copy-start = (bf16[1024,1024]{1,0:T(8,128)(2,1)S(1)}, bf16[1024,1024]{1,0:T(8,128)(2,1)}, u32[]{:S(2)}) copy-start(bf16[1024,1024]{1,0:T(8,128)(2,1)} %param.16) | copy-start | bytes 6291460
  17.9 89.8 %copy-start.4 = (f32[8,128]{1,0:T(8,128)S(1)}, f32[8,128]{1,0:T(8,128)}, u32[]{:S(2)}) copy-start(f32[8,128]{1,0:T(8,128)} %param.17) | copy-start | bytes 12292
  110.2 2.9 copy-start.1
  110.2 3.5 %copy-start.2 = (bf16[2048,512]{1,0:T(8,128)(2,1)S(1)}, bf16[2048,512]{1,0:T(8,128)(2,1)}, u32[]{:S(2)}) copy-start(bf16[2048,512]{1,0:T(8,128)(2,1)} %get-tuple-element.18) | copy-start | bytes 6291460
  287.3 1.0 copy-start.3

commit v2 on v1

--- a/solution.py
+++ b/solution.py
@@ -197,42 +197,40 @@
         started.append(copy)
         return copy
 
-    z_copies = [None]
-    for j in range(1, zs):
-        z_copies.append(go(qall.at[mine], z_send.at[j], z_recv.at[j], (req, lax.rem(z + j, zs))))
+    spans = (first, second)
+    z_copies = {}
+    for h in range(2):
+        for j in range(1, zs):
+            z_copies[h, j] = go(
+                qall.at[mine, spans[h], :], z_send.at[h, j], z_recv.at[h, j],
+                (req, lax.rem(z + j, zs)),
+            )
     hops = []
     forwards = []
-    for j in range(zs + 1):
-        if j < zs:
-            zz = lax.rem(z - j + zs, zs)
+    order = [(0, 0), (1, 0)] + [(h, j) for h in range(2) for j in range(1, zs)]
+    for step in range(len(order) + 1):
+        if step < len(order):
+            h, j = order[step]
             if j > 0:
-                z_copies[j].wait_recv()
-            here = slot(zz, y, x)
-            hops.append((
-                go(qall.at[here, first, :], a_send.at[0, j], a_recv.at[0, j], yn),
-                go(qall.at[here, second, :], a_send.at[1, j], a_recv.at[1, j], xn),
-            ))
+                z_copies[h, j].wait_recv()
+            here = slot(lax.rem(z - j + zs, zs), y, x)
+            near, far = (yn, xn) if h == 0 else (xn, yn)
+            hops.append(go(qall.at[here, spans[h], :], a_send.at[h, j], a_recv.at[h, j], near))
             forwards.append(
-                go(qall.at[here, first, :], e_send.at[0, j], e_recv.at[0, j], xn)
+                go(qall.at[here, spans[h], :], e_send.at[h, j], e_recv.at[h, j], far)
             )
-            forwards.append(
-                go(qall.at[here, second, :], e_send.at[1, j], e_recv.at[1, j], yn)
-            )
-        if j == 0:
+        if step == 1:
             for copy in metas:
                 copy.start()
             for copy in pair[1:]:
                 copy.start()
-        if j > 0:
-            i = j - 1
-            zz = lax.rem(z - i + zs, zs)
-            hops[i][0].wait_recv()
+        if step > 0:
+            h, j = order[step - 1]
+            zz = lax.rem(z - j + zs, zs)
+            away = slot(zz, 1 - y, x) if h == 0 else slot(zz, y, 1 - x)
+            hops[step - 1].wait_recv()
             forwards.append(
-                go(qall.at[slot(zz, 1 - y, x), first, :], f_send.at[0, i], f_recv.at[0, i], xn)
-            )
-            hops[i][1].wait_recv()
-            forwards.append(
-                go(qall.at[slot(zz, y, 1 - x), second, :], f_send.at[1, i], f_recv.at[1, i], yn)
+                go(qall.at[away, spans[h], :], f_send.at[h, j], f_recv.at[h, j], xn if h == 0 else yn)
             )
     for copy in forwards:
         copy.wait_recv()
@@ -264,7 +262,7 @@
         out_specs=(ANY,) * 4,
         scratch_shapes=[
             dma((2,)), dma((4,)), dma((4,)), dma((devices - 1,)), dma((devices - 1,)),
-            dma((zs,)), dma((zs,)), dma((2, zs)), dma((2, zs)), dma((2, zs)), dma((2, zs)),
+            dma((2, zs)), dma((2, zs)), dma((2, zs)), dma((2, zs)), dma((2, zs)), dma((2, zs)),
             dma((2, zs)), dma((2, zs)),
         ],
         compiler_params=pltpu.CompilerParams(collective_id=0, has_side_effects=True),
@@ -374,7 +372,8 @@
     windows = (pl.ds(0, rows), pl.ds(rows, rows))
     order = list(range(1, zs)) + [0]
     firsts, seconds, z_copies = {}, {}, {}
-    for j in order:
+
+    def begin(j):
         zz = lax.rem(z + j, zs)
         for k in range(2):
             for keep in (0, 1):
@@ -396,6 +395,9 @@
                     )
                     copy.start()
                     firsts[j, h, keep] = copy
+
+    begin(order[0])
+    begin(order[1])
     for step in range(len(order) + 1):
         if step < len(order):
             j = order[step]
@@ -411,6 +413,8 @@
                 )
                 copy.start()
                 seconds[j, h] = copy
+            if step + 2 < len(order):
+                begin(order[step + 2])
         if step > 0:
             j = order[step - 1]
             zz = lax.rem(z + j, zs)

time: 290 us -> 263 us (0.907)
  Pallas kernels: 257 us -> 228 us
    pallas_call x1, Pallas kernels: 123 us -> 88.1 us  [collect(): pl.pallas_call(collect_kernel, out_shape=(jax.ShapeDtypeStruct((rows, col...]
    pallas_call x1, Pallas kernels: 87.3 us -> 92.9 us  [spread(): pl.pallas_call(spread_kernel, out_shape=(jax.ShapeDtypeStruct((devices //...]
where the time goes in v2:
time: 263 us; the launch traced here: 260 us
  Pallas kernels  228 us (87%)
  local copies, waits for them, and re-layouts  15.8 us (6%)
  other arithmetic  9.8 us (4%)
  matrix products  6.12 us (2%)
    pallas_call x1, Pallas kernels, spread(): pl.pallas_call(spread_kernel, out_shape=(jax.ShapeDtypeStruct((devices //...  92.9 us
    pallas_call x1, Pallas kernels, collect(): pl.pallas_call(collect_kernel, out_shape=(jax.ShapeDtypeStruct((rows, col...  88.1 us
    pallas_call x1, Pallas kernels, attend(): pl.pallas_call(functools.partial(attend_kernel, scale), out_shape=jax.Sha...  46.6 us

profile of v2, /device:TPU:9, one launch (start us, length us, event | category | flops | bytes accessed | tf_op | source)
XLA Modules:
  0.0 260.3 jit_solution(5016825461096621296)
XLA Ops:
  0.8 0.8 select_reduce_fusion
  1.6 0.9 convert_reduce_fusion.1
  2.5 0.7 multiply_add_fusion
  3.2 1.2 convert_reduce_fusion
  4.4 1.3 fusion.5
  6.4 0.8 copy.25
  7.2 0.9 copy.23
  8.1 0.7 reshape.82.bucket_ref
  8.8 3.8 %multiply_convert_fusion = bf16[256,2048]{1,0:T(8,128)(2,1)S(1)} fusion(bf16[1024,2048]{1,0:T(8,128)(2,1)} %param.15, bf16[256,1024]{1,0:T(8,128)(2,1)} %param.9, f32[256]{0:T(256)S(1)} %add_rsqrt_fusion.1, f32[256]{0:T(256)S(1)} %broadcast_multiply_fusion.1), kind=kOutput, calls=%fused_computation.4 | convolution fusion | flops 1077411840 | bytes 5769216 | tf_op jit(solution)/shard_map/dot_general | solution.py:21
  12.6 0.8 slice.24.q_ref
  13.4 4.5 %constant_dynamic-slice_fusion = (bf16[2048,512]{1,0:T(8,128)(2,1)}, bf16[2048,512]{1,0:T(8,128)(2,1)}) fusion(bf16[2048,2048]{1,0:T(8,128)(2,1)} %bitcast.32, s32[]{:T(128)S(6)} %select_n.25, s32[]{:T(128)S(6)} %select_n.24), kind=kLoop, calls=%fused_computation.42 | loop fusion | bytes 8388616 | tf_op jit(solution)/shard_map/dynamic_slice | solution.py:540
  17.9 92.9 %shard_map.91 = (bf16[16,512,512]{2,1,0:T(8,128)(2,1)}, bf16[2,2048,512]{2,1,0:T(8,128)(2,1)}, s32[32,8,128]{2,1,0:T(8,128)}, s32[16,128]{1,0:T(8,128)}) custom-call(bf16[256,1024]{1,0:T(8,128)(2,1)} %slice.24.q_ref, bf16[2048,2048]{1,0:T(8,128)(2,1)} %bitcast.33, s32[8,128]{1,0:T(8,128)} %add_bitcast_fusion.1.meta_ref, s32[16,128]{1,0:T(8,128)} %reshape.82.bucket_ref), custom_call_target="tpu_custom_call" | custom-call | tf_op jit(solution)/shard_map/pallas_call | solution.py:253
  110.8 0.9 copy.32
  111.8 0.7 reshape.85.slot_ref
  112.5 0.8 reshape.89
  113.3 0.8 fusion.4
  114.1 0.7 reshape.91.bias_ref
  115.2 0.7 reshape.96.live_ref
  115.8 2.7 %fusion.22 = (bf16[1,2048,512]{2,1,0:T(8,128)(2,1)S(1)}, bf16[1,2048,512]{2,1,0:T(8,128)(2,1)S(1)}) fusion(bf16[2,2048,512]{2,1,0:T(8,128)(2,1)} %get-tuple-element.13), kind=kLoop, calls=%fused_computation.51 | loop fusion | bytes 8388608 | tf_op jit(solution)/shard_map/slice | solution.py:550
  118.7 0.6 copy-done.2
  119.3 3.7 %pad_maximum_fusion = (bf16[32,128,512]{2,1,0:T(8,128)(2,1)}, bf16[32,128,512]{2,1,0:T(8,128)(2,1)}) fusion(bf16[32,64,512]{2,1,0:T(8,128)(2,1)S(1)} %bitcast.37, bf16[32,64,512]{2,1,0:T(8,128)(2,1)S(1)} %bitcast.35, bf16[32,64,512]{2,1,0:T(8,128)(2,1)S(1)} %bitcast.36, bf16[32,64,512]{2,1,0:T(8,128)(2,1)S(1)} %bitcast.34), kind=kLoop, calls=%fused_computation.1 | loop fusion | flops 16777216 | bytes 16777216 | tf_op jit(solution)/shard_map/concatenate | solution.py:541
  123.0 46.6 %shard_map.92.part = bf16[16,512,512]{2,1,0:T(8,128)(2,1)} custom-call(bf16[16,512,512]{2,1,0:T(8,128)(2,1)} %get-tuple-element.11.q_ref, s32[32,1,256]{2,1,0:T(1,128)} %reshape.85.slot_ref, bf16[32,128,512]{2,1,0:T(8,128)(2,1)} %get-tuple-element.25.k_ref, bf16[32,128,512]{2,1,0:T(8,128)(2,1)} %get-tuple-element.26.v_ref, f32[32,2,256]{2,1,0:T(2,128)} %reshape.91.bias_ref, ...), custom_call_target="tpu_custom_call" | custom-call | flops 20000000000 | bytes 25165824 | tf_op jit(solution)/shard_map/pallas_call | solution.py:342
  169.6 88.1 %shard_map.93 = (f32[256,512]{1,0:T(8,128)S(1)}, f32[256,512]{1,0:T(8,128)S(1)}) custom-call(bf16[16,512,512]{2,1,0:T(8,128)(2,1)} %shard_map.92.part), custom_call_target="tpu_custom_call" | custom-call | tf_op jit(solution)/shard_map/pallas_call | solution.py:456
  258.8 1.6 fusion.1
  (33 shorter events, 2.4 us)
Async XLA Ops:
  0.0 258.2 %copy-start = (bf16[1024,1024]{1,0:T(8,128)(2,1)S(1)}, bf16[1024,1024]{1,0:T(8,128)(2,1)}, u32[]{:S(2)}) copy-start(bf16[1024,1024]{1,0:T(8,128)(2,1)} %param.16) | copy-start | bytes 6291460
  17.9 95.4 %copy-start.4 = (f32[8,128]{1,0:T(8,128)S(1)}, f32[8,128]{1,0:T(8,128)}, u32[]{:S(2)}) copy-start(f32[8,128]{1,0:T(8,128)} %param.17) | copy-start | bytes 12292
  115.8 2.9 %copy-start.1 = (bf16[2048,512]{1,0:T(8,128)(2,1)S(1)}, bf16[2048,512]{1,0:T(8,128)(2,1)}, u32[]{:S(2)}) copy-start(bf16[2048,512]{1,0:T(8,128)(2,1)} %get-tuple-element.17) | copy-start | bytes 6291460
  115.8 3.5 %copy-start.2 = (bf16[2048,512]{1,0:T(8,128)(2,1)S(1)}, bf16[2048,512]{1,0:T(8,128)(2,1)}, u32[]{:S(2)}) copy-start(bf16[2048,512]{1,0:T(8,128)(2,1)} %get-tuple-element.18) | copy-start | bytes 6291460
  257.7 1.0 copy-start.3
